TPU v7x, 512 devices: a whole 4x8x8 slice. The times are simulated.
512 devices in a mesh: depth: 8 (over y), lat: 32 (over z, x), freq: 2 (over core).
Axes of the slice: x: 4, y: 8, z: 8, core: 2. Of those that a mesh axis runs over, the one named last changes fastest.
Arguments:
- surface: bfloat16 [6, 2, 128, 32768], P('freq', None, None, 'lat'), may hold values from -6 to 6
- refl: float32 [8, 32768], P('depth', 'lat'), may hold values from -0.5 to 0.5
- pool: bfloat16 [8, 6, 8, 128, 256], P('depth', 'freq'), may hold values from -0.375 to 0.375
- tile_ids: int32 [8, 256, 10], P('depth', 'lat'), may hold values from 0 to 255, as said below
- block_ids: int32 [8, 256, 10], P('depth', 'lat'), may hold values from 0 to 7
- counts: int32 [8, 256], P('depth', 'lat'), may hold values from 1 to 10, as said below
Outputs:
- image: float32 [8, 32768], P('depth', 'lat')
Inputs may be any that keep to these rules, and one draw needn't show every extreme that they name: tile_ids[l, j, k] = (j + o) mod 256 for an offset o with -8 <= o <= 8; slot 0 names the row's own tile; in every level some row has all 10 slots live with offsets 8 at slot 1 and -8 at slot 2. Slots k >= counts[l, j] of row j are padding; in every level some row has all 10 slots live.
All inputs are finite; a program needn't handle non-finite values.
Results may differ from a plain program's by a relative error of at most 0.00055.
Values may be sent and summed in bfloat16 or wider, within the bound.
A program may use at most 128 MiB of HBM per device.

v0:
```python
import jax
import jax.numpy as jnp
from jax import lax
from jax.sharding import PartitionSpec as P

TILE = 128
TILE_DEV = 8


def extended_2(block, sides, width):
    for axis, dim in sides:
        count = lax.axis_size(axis)
        forward = [(i, i + 1) for i in range(count - 1)]
        forward.append((count - 1, 0))
        backward = [(target, source) for source, target in forward]
        low = lax.ppermute(
            lax.slice_in_dim(block, block.shape[dim] - width, None, axis=dim), axis, forward
        )
        high = lax.ppermute(lax.slice_in_dim(block, 0, width, axis=dim), axis, backward)
        block = jnp.concatenate([low, block, high], axis=dim)
    return block


def in_one_piece(arrays, axis, dim, along):
    columns = [a.reshape(*a.shape[:along], -1) for a in arrays]
    both = jnp.concatenate(columns, axis=along)
    whole, at, gathered = (lax.all_gather(both, axis, axis=dim, tiled=True), 0, [])
    for a, column in zip(arrays, columns):
        piece = whole[..., at : at + column.shape[along]]
        gathered.append(piece.reshape(*piece.shape[:along], *a.shape[along:]))
        at += column.shape[along]
    return tuple(gathered)


def copy_for_each(shard, axis):
    copies = jnp.broadcast_to(shard, (lax.axis_size(axis), *shard.shape))
    return lax.all_to_all(copies, axis, split_axis=0, concat_axis=0, tiled=True)


def in_order(parts, dim):
    parts = jnp.moveaxis(parts, 0, dim)
    shape = parts.shape
    return parts.reshape(*shape[:dim], shape[dim] * shape[dim + 1], *shape[dim + 2 :])


def gather_directly(shard, axis, dim):
    parts = copy_for_each(shard, axis)
    return in_order(parts, dim)


def cut_along(shard, dim, length):
    before, after = (shard.shape[:dim], shard.shape[dim + 1 :])
    return jnp.moveaxis(shard.reshape(*before, length, -1, *after), dim, 0)


def summed_on_arrival(shard, axis, dim):
    parts = cut_along(shard, dim, lax.axis_size(axis))
    arrived = lax.all_to_all(parts, axis, split_axis=0, concat_axis=0, tiled=True)
    return arrived.sum(axis=0)


def aperture_rim(wave_field):
    return extended_2(wave_field, (("lat", 3),), TILE_DEV * TILE)


def extrapolate(extended, pool_level, local_ids, block_level, count_level, refl_level):
    freqs_here = extended.shape[0]
    shot_rows = extended.shape[2]
    tile_rows = local_ids.shape[0]
    slot_total = local_ids.shape[1]
    tile_grid = extended.reshape(freqs_here, 2, shot_rows, -1, TILE)
    slot_live = (jnp.arange(slot_total)[None, :] < count_level[:, None]).astype(jnp.bfloat16)
    picked = jnp.take(tile_grid, local_ids, axis=3) * slot_live[None, None, None, :, :, None]
    chosen = jnp.take(pool_level, block_level, axis=1)
    product = jnp.einsum("fsarkt,frktc->rfsac", picked, chosen, preferred_element_type=jnp.float32)
    real_part = product[:, :, 0, :, :TILE] - product[:, :, 1, :, TILE:]
    imag_part = product[:, :, 0, :, TILE:] + product[:, :, 1, :, :TILE]
    row_scale = 1.0 / jnp.sqrt(count_level.astype(jnp.float32))
    rows_out = jnp.stack([real_part, imag_part], 2) * row_scale[:, None, None, None, None]
    wave_out = jnp.transpose(rows_out, (1, 2, 3, 0, 4)).reshape(
        freqs_here, 2, shot_rows, tile_rows * TILE
    )
    wave_out = wave_out * (1.0 - refl_level)
    return (wave_out.astype(jnp.bfloat16), jnp.sum(wave_out * wave_out, axis=(0, 1, 2)))


def per_device(surface, refl, pool, tile_ids, block_ids, counts):
    depth_index = lax.axis_index("depth")
    lat_index = lax.axis_index("lat")
    tile_count = TILE_DEV * lax.axis_size("lat")
    first_tile = lat_index * TILE_DEV - TILE_DEV
    freqs_here = surface.shape[0]
    shot_total = surface.shape[2]
    lateral_width = surface.shape[3]
    shot_rows = shot_total // lax.axis_size("depth")
    own_shots = lax.dynamic_slice_in_dim(surface, depth_index * shot_rows, shot_rows, 2)
    pool_all = lax.all_gather(pool, "depth", axis=0, tiled=True)
    ids_all, blocks_all, counts_all = in_one_piece((tile_ids, block_ids, counts), "depth", 0, 2)
    refl_all = gather_directly(refl, "depth", 0)
    level_total = pool_all.shape[0]

    def level_step(level_index, loop_state):
        wave_field, images = loop_state
        ids_here = lax.dynamic_index_in_dim(ids_all, level_index, 0, keepdims=False)
        local_level = jnp.mod(ids_here - first_tile, tile_count)
        pool_here = lax.dynamic_index_in_dim(pool_all, level_index, 0, keepdims=False)
        blocks_here = lax.dynamic_index_in_dim(blocks_all, level_index, 0, keepdims=False)
        counts_here = lax.dynamic_index_in_dim(counts_all, level_index, 0, keepdims=False)
        refl_here = lax.dynamic_index_in_dim(refl_all, level_index, 0, keepdims=False)
        handed, partial_value = extrapolate(
            aperture_rim(wave_field), pool_here, local_level, blocks_here, counts_here, refl_here
        )
        images = lax.dynamic_update_index_in_dim(images, partial_value, level_index, 0)
        return (handed, images)

    start_images = jnp.zeros((level_total, lateral_width), jnp.float32)
    loop_state = lax.fori_loop(0, level_total, level_step, (own_shots, start_images))
    image_local = summed_on_arrival(loop_state[1], "depth", 0)[0]
    summed = lax.psum(image_local, "freq")
    divisor = freqs_here * lax.axis_size("freq") * shot_total
    return (summed / divisor)[None, :]


def solution(mesh):
    placed = (
        P("freq", None, None, "lat"),
        P("depth", "lat"),
        P("depth", "freq", None, None, None),
        P("depth", "lat", None),
        P("depth", "lat", None),
        P("depth", "lat"),
    )
    return jax.shard_map(
        per_device, mesh=mesh, in_specs=placed, out_specs=P("depth", "lat"), check_vma=False
    )
```

profile of v0, /device:TPU:1, one launch (start us, length us, event | category | flops | bytes accessed | tf_op | source)
XLA Modules:
  0.0 460.4 jit_solution(3497054629939524282)
XLA Ops:
  8.6 7.7 %all-to-all-start = ((f32[8,1,1024]{2,1,0:T(1,128)}), f32[8,1,1024]{2,1,0:T(1,128)S(1)}, u32[]{:S(2)}, u32[]{:S(2)}) async-start(f32[8,1,1024]{2,1,0:T(1,128)} %broadcast_in_dim.88), calls=%async_computation | async-start | bytes 65536 | tf_op jit(solution)/shard_map/all_to_all | solution.py:37
  17.7 20.8 %all_gather.6 = s32[8,8,21]{2,1,0:T(8,128)S(1)} all-gather(s32[1,8,21]{2,1,0:T(8,128)S(1)} %pad_add_fusion), channel_id=1, replica_groups=mesh['depth'=8,'lat'=32,'freq'=2] {'depth'}, dimensions={0}, use_global_device_ids=true | all-gather | bytes 6048 | tf_op jit(solution)/shard_map/all_gather | solution.py:27
  40.0 110.9 %all-gather.2.cloned.1.call-done = bf16[8,3,8,128,256]{4,3,2,1,0:T(8,128)(2,1)} async-done(((bf16[1,3,8,128,256]{4,3,2,1,0:T(8,128)(2,1)}), bf16[8,3,8,128,256]{4,3,2,1,0:T(8,128)(2,1)}) %all-gather.2.cloned.1.call-update) | async-done | bytes 12582928 | tf_op jit(solution)/shard_map/all_gather | solution.py:97
  150.9 281.9 %while.17 = (s32[]{:T(128)}, bf16[3,2,16,1024]{3,2,1,0:T(8,128)(2,1)S(1)}, f32[8,1024]{1,0:T(8,128)}, s32[8,8,10]{2,1,0:T(8,128)S(1)}, s32[]{:T(128)}, /*index=5...) while((s32[]{:T(128)}, ...), condition=%wide.region_2.3_spmd, body=%wide.region_0.2_spmd.sunk | while | flops 515904960 | bytes 62015692 | solution.py:117
  150.9 7.8 %collective-permute-start = (bf16[3,2,16,1024]{3,2,1,0:T(8,128)(2,1)S(1)}, bf16[3,2,16,1024]{3,2,1,0:T(8,128)(2,1)S(1)}, u32[]{:S(2)}, u32[]{:S(2)}) collective-permute-start(bf16[3,2,16,1024]{3,2,1,0:T(8,128)(2,1)S(1)} %get-tuple-element.365), channel_id=1, source_target_pairs={{2,0},{4,2},{6,4},{8,6},{10,8},{12,10},{14,12},{16,14},{18,16},{20... | collective-permute-start | bytes 589832 | tf_op jit(solution)/shard_map/while/body/eval_jaxpr/ppermute | solution.py:19
  158.7 1.9 collective-permute-start.1
  161.3 1.5 dynamic-slice_bitcast_fusion.2
  164.9 8.1 %gather_fusion = bf16[80,3,128,256]{3,2,1,0:T(8,128)(2,1)} fusion(bf16[3,8,128,256]{3,2,1,0:T(8,128)(2,1)S(1)} %dynamic-slice_bitcast_fusion.2, s32[1024]{0:T(1024)S(1)} %pad_clamp_fusion.4), kind=kCustom, calls=%fused_computation.1.clone.1 | custom fusion | bytes 31457600 | tf_op jit(solution)/shard_map/while/body/eval_jaxpr/jit(_take)/gather | solution.py:74
  174.8 2.4 gather_fusion.1
  177.3 8.0 %fusion.30 = f32[8,3,2,16,256]{4,3,2,1,0:T(8,128)S(1)} fusion(bf16[8,10,3,128,256]{4,3,2,1,0:T(8,128)(2,1)} %bitcast.98, pred[8,10]{1,0:T(8,128)(4,1)S(1)} %copy-done.5, bf16[8,10,3,2,16,128]{5,4,3,2,1,0:T(8,128)(2,1)} %bitcast.99, pred[8,10]{1,0:T(8,128)(4,1)S(1)} %copy-done.6, bf16[8,10]{1,0:T(8,128)(2,1)S(1)} %fusion.29), kind=kOutput, calls=%fused_computation.8.clone.1 | convolution fusion | flops 513146880 | bytes 18481472 | tf_op jit(solution)/shard_map/while/body/eval_jaxpr/fsarkt,frktc->rfsac/dot_general | solution.py:75
  187.1 6.7 %collective-permute-start = (bf16[3,2,16,1024]{3,2,1,0:T(8,128)(2,1)S(1)}, bf16[3,2,16,1024]{3,2,1,0:T(8,128)(2,1)S(1)}, u32[]{:S(2)}, u32[]{:S(2)}) collective-permute-start(bf16[3,2,16,1024]{3,2,1,0:T(8,128)(2,1)S(1)} %get-tuple-element.365), channel_id=1, source_target_pairs={{2,0},{4,2},{6,4},{8,6},{10,8},{12,10},{14,12},{16,14},{18,16},{20... | collective-permute-start | bytes 589832 | tf_op jit(solution)/shard_map/while/body/eval_jaxpr/ppermute | solution.py:19
  193.8 1.9 collective-permute-start.1
  196.4 1.5 dynamic-slice_bitcast_fusion.2
  200.1 8.2 %gather_fusion = bf16[80,3,128,256]{3,2,1,0:T(8,128)(2,1)} fusion(bf16[3,8,128,256]{3,2,1,0:T(8,128)(2,1)S(1)} %dynamic-slice_bitcast_fusion.2, s32[1024]{0:T(1024)S(1)} %pad_clamp_fusion.4), kind=kCustom, calls=%fused_computation.1.clone.1 | custom fusion | bytes 31457600 | tf_op jit(solution)/shard_map/while/body/eval_jaxpr/jit(_take)/gather | solution.py:74
  210.0 2.4 gather_fusion.1
  212.4 8.0 %fusion.30 = f32[8,3,2,16,256]{4,3,2,1,0:T(8,128)S(1)} fusion(bf16[8,10,3,128,256]{4,3,2,1,0:T(8,128)(2,1)} %bitcast.98, pred[8,10]{1,0:T(8,128)(4,1)S(1)} %copy-done.5, bf16[8,10,3,2,16,128]{5,4,3,2,1,0:T(8,128)(2,1)} %bitcast.99, pred[8,10]{1,0:T(8,128)(4,1)S(1)} %copy-done.6, bf16[8,10]{1,0:T(8,128)(2,1)S(1)} %fusion.29), kind=kOutput, calls=%fused_computation.8.clone.1 | convolution fusion | flops 513146880 | bytes 18481472 | tf_op jit(solution)/shard_map/while/body/eval_jaxpr/fsarkt,frktc->rfsac/dot_general | solution.py:75
  222.2 6.7 %collective-permute-start = (bf16[3,2,16,1024]{3,2,1,0:T(8,128)(2,1)S(1)}, bf16[3,2,16,1024]{3,2,1,0:T(8,128)(2,1)S(1)}, u32[]{:S(2)}, u32[]{:S(2)}) collective-permute-start(bf16[3,2,16,1024]{3,2,1,0:T(8,128)(2,1)S(1)} %get-tuple-element.365), channel_id=1, source_target_pairs={{2,0},{4,2},{6,4},{8,6},{10,8},{12,10},{14,12},{16,14},{18,16},{20... | collective-permute-start | bytes 589832 | tf_op jit(solution)/shard_map/while/body/eval_jaxpr/ppermute | solution.py:19
  228.9 1.9 collective-permute-start.1
  235.1 8.1 %gather_fusion = bf16[80,3,128,256]{3,2,1,0:T(8,128)(2,1)} fusion(bf16[3,8,128,256]{3,2,1,0:T(8,128)(2,1)S(1)} %dynamic-slice_bitcast_fusion.2, s32[1024]{0:T(1024)S(1)} %pad_clamp_fusion.4), kind=kCustom, calls=%fused_computation.1.clone.1 | custom fusion | bytes 31457600 | tf_op jit(solution)/shard_map/while/body/eval_jaxpr/jit(_take)/gather | solution.py:74
  245.1 2.4 gather_fusion.1
  247.5 8.0 %fusion.30 = f32[8,3,2,16,256]{4,3,2,1,0:T(8,128)S(1)} fusion(bf16[8,10,3,128,256]{4,3,2,1,0:T(8,128)(2,1)} %bitcast.98, pred[8,10]{1,0:T(8,128)(4,1)S(1)} %copy-done.5, bf16[8,10,3,2,16,128]{5,4,3,2,1,0:T(8,128)(2,1)} %bitcast.99, pred[8,10]{1,0:T(8,128)(4,1)S(1)} %copy-done.6, bf16[8,10]{1,0:T(8,128)(2,1)S(1)} %fusion.29), kind=kOutput, calls=%fused_computation.8.clone.1 | convolution fusion | flops 513146880 | bytes 18481472 | tf_op jit(solution)/shard_map/while/body/eval_jaxpr/fsarkt,frktc->rfsac/dot_general | solution.py:75
  257.3 6.7 %collective-permute-start = (bf16[3,2,16,1024]{3,2,1,0:T(8,128)(2,1)S(1)}, bf16[3,2,16,1024]{3,2,1,0:T(8,128)(2,1)S(1)}, u32[]{:S(2)}, u32[]{:S(2)}) collective-permute-start(bf16[3,2,16,1024]{3,2,1,0:T(8,128)(2,1)S(1)} %get-tuple-element.365), channel_id=1, source_target_pairs={{2,0},{4,2},{6,4},{8,6},{10,8},{12,10},{14,12},{16,14},{18,16},{20... | collective-permute-start | bytes 589832 | tf_op jit(solution)/shard_map/while/body/eval_jaxpr/ppermute | solution.py:19
  264.0 1.9 collective-permute-start.1
  270.3 8.2 %gather_fusion = bf16[80,3,128,256]{3,2,1,0:T(8,128)(2,1)} fusion(bf16[3,8,128,256]{3,2,1,0:T(8,128)(2,1)S(1)} %dynamic-slice_bitcast_fusion.2, s32[1024]{0:T(1024)S(1)} %pad_clamp_fusion.4), kind=kCustom, calls=%fused_computation.1.clone.1 | custom fusion | bytes 31457600 | tf_op jit(solution)/shard_map/while/body/eval_jaxpr/jit(_take)/gather | solution.py:74
  280.2 2.4 gather_fusion.1
  282.7 8.0 %fusion.30 = f32[8,3,2,16,256]{4,3,2,1,0:T(8,128)S(1)} fusion(bf16[8,10,3,128,256]{4,3,2,1,0:T(8,128)(2,1)} %bitcast.98, pred[8,10]{1,0:T(8,128)(4,1)S(1)} %copy-done.5, bf16[8,10,3,2,16,128]{5,4,3,2,1,0:T(8,128)(2,1)} %bitcast.99, pred[8,10]{1,0:T(8,128)(4,1)S(1)} %copy-done.6, bf16[8,10]{1,0:T(8,128)(2,1)S(1)} %fusion.29), kind=kOutput, calls=%fused_computation.8.clone.1 | convolution fusion | flops 513146880 | bytes 18481472 | tf_op jit(solution)/shard_map/while/body/eval_jaxpr/fsarkt,frktc->rfsac/dot_general | solution.py:75
  292.4 6.7 %collective-permute-start = (bf16[3,2,16,1024]{3,2,1,0:T(8,128)(2,1)S(1)}, bf16[3,2,16,1024]{3,2,1,0:T(8,128)(2,1)S(1)}, u32[]{:S(2)}, u32[]{:S(2)}) collective-permute-start(bf16[3,2,16,1024]{3,2,1,0:T(8,128)(2,1)S(1)} %get-tuple-element.365), channel_id=1, source_target_pairs={{2,0},{4,2},{6,4},{8,6},{10,8},{12,10},{14,12},{16,14},{18,16},{20... | collective-permute-start | bytes 589832 | tf_op jit(solution)/shard_map/while/body/eval_jaxpr/ppermute | solution.py:19
  299.1 1.9 collective-permute-start.1
  305.4 8.1 %gather_fusion = bf16[80,3,128,256]{3,2,1,0:T(8,128)(2,1)} fusion(bf16[3,8,128,256]{3,2,1,0:T(8,128)(2,1)S(1)} %dynamic-slice_bitcast_fusion.2, s32[1024]{0:T(1024)S(1)} %pad_clamp_fusion.4), kind=kCustom, calls=%fused_computation.1.clone.1 | custom fusion | bytes 31457600 | tf_op jit(solution)/shard_map/while/body/eval_jaxpr/jit(_take)/gather | solution.py:74
  315.3 2.4 gather_fusion.1
  317.7 8.0 %fusion.30 = f32[8,3,2,16,256]{4,3,2,1,0:T(8,128)S(1)} fusion(bf16[8,10,3,128,256]{4,3,2,1,0:T(8,128)(2,1)} %bitcast.98, pred[8,10]{1,0:T(8,128)(4,1)S(1)} %copy-done.5, bf16[8,10,3,2,16,128]{5,4,3,2,1,0:T(8,128)(2,1)} %bitcast.99, pred[8,10]{1,0:T(8,128)(4,1)S(1)} %copy-done.6, bf16[8,10]{1,0:T(8,128)(2,1)S(1)} %fusion.29), kind=kOutput, calls=%fused_computation.8.clone.1 | convolution fusion | flops 513146880 | bytes 18481472 | tf_op jit(solution)/shard_map/while/body/eval_jaxpr/fsarkt,frktc->rfsac/dot_general | solution.py:75
  327.5 6.7 %collective-permute-start = (bf16[3,2,16,1024]{3,2,1,0:T(8,128)(2,1)S(1)}, bf16[3,2,16,1024]{3,2,1,0:T(8,128)(2,1)S(1)}, u32[]{:S(2)}, u32[]{:S(2)}) collective-permute-start(bf16[3,2,16,1024]{3,2,1,0:T(8,128)(2,1)S(1)} %get-tuple-element.365), channel_id=1, source_target_pairs={{2,0},{4,2},{6,4},{8,6},{10,8},{12,10},{14,12},{16,14},{18,16},{20... | collective-permute-start | bytes 589832 | tf_op jit(solution)/shard_map/while/body/eval_jaxpr/ppermute | solution.py:19
  334.2 1.9 collective-permute-start.1
  340.5 8.2 %gather_fusion = bf16[80,3,128,256]{3,2,1,0:T(8,128)(2,1)} fusion(bf16[3,8,128,256]{3,2,1,0:T(8,128)(2,1)S(1)} %dynamic-slice_bitcast_fusion.2, s32[1024]{0:T(1024)S(1)} %pad_clamp_fusion.4), kind=kCustom, calls=%fused_computation.1.clone.1 | custom fusion | bytes 31457600 | tf_op jit(solution)/shard_map/while/body/eval_jaxpr/jit(_take)/gather | solution.py:74
  350.5 2.4 gather_fusion.1
  352.9 8.0 %fusion.30 = f32[8,3,2,16,256]{4,3,2,1,0:T(8,128)S(1)} fusion(bf16[8,10,3,128,256]{4,3,2,1,0:T(8,128)(2,1)} %bitcast.98, pred[8,10]{1,0:T(8,128)(4,1)S(1)} %copy-done.5, bf16[8,10,3,2,16,128]{5,4,3,2,1,0:T(8,128)(2,1)} %bitcast.99, pred[8,10]{1,0:T(8,128)(4,1)S(1)} %copy-done.6, bf16[8,10]{1,0:T(8,128)(2,1)S(1)} %fusion.29), kind=kOutput, calls=%fused_computation.8.clone.1 | convolution fusion | flops 513146880 | bytes 18481472 | tf_op jit(solution)/shard_map/while/body/eval_jaxpr/fsarkt,frktc->rfsac/dot_general | solution.py:75
  362.7 6.6 %collective-permute-start = (bf16[3,2,16,1024]{3,2,1,0:T(8,128)(2,1)S(1)}, bf16[3,2,16,1024]{3,2,1,0:T(8,128)(2,1)S(1)}, u32[]{:S(2)}, u32[]{:S(2)}) collective-permute-start(bf16[3,2,16,1024]{3,2,1,0:T(8,128)(2,1)S(1)} %get-tuple-element.365), channel_id=1, source_target_pairs={{2,0},{4,2},{6,4},{8,6},{10,8},{12,10},{14,12},{16,14},{18,16},{20... | collective-permute-start | bytes 589832 | tf_op jit(solution)/shard_map/while/body/eval_jaxpr/ppermute | solution.py:19
  369.3 1.9 collective-permute-start.1
  375.6 8.2 %gather_fusion = bf16[80,3,128,256]{3,2,1,0:T(8,128)(2,1)} fusion(bf16[3,8,128,256]{3,2,1,0:T(8,128)(2,1)S(1)} %dynamic-slice_bitcast_fusion.2, s32[1024]{0:T(1024)S(1)} %pad_clamp_fusion.4), kind=kCustom, calls=%fused_computation.1.clone.1 | custom fusion | bytes 31457600 | tf_op jit(solution)/shard_map/while/body/eval_jaxpr/jit(_take)/gather | solution.py:74
  385.5 2.4 gather_fusion.1
  387.9 8.0 %fusion.30 = f32[8,3,2,16,256]{4,3,2,1,0:T(8,128)S(1)} fusion(bf16[8,10,3,128,256]{4,3,2,1,0:T(8,128)(2,1)} %bitcast.98, pred[8,10]{1,0:T(8,128)(4,1)S(1)} %copy-done.5, bf16[8,10,3,2,16,128]{5,4,3,2,1,0:T(8,128)(2,1)} %bitcast.99, pred[8,10]{1,0:T(8,128)(4,1)S(1)} %copy-done.6, bf16[8,10]{1,0:T(8,128)(2,1)S(1)} %fusion.29), kind=kOutput, calls=%fused_computation.8.clone.1 | convolution fusion | flops 513146880 | bytes 18481472 | tf_op jit(solution)/shard_map/while/body/eval_jaxpr/fsarkt,frktc->rfsac/dot_general | solution.py:75
  397.7 6.7 %collective-permute-start = (bf16[3,2,16,1024]{3,2,1,0:T(8,128)(2,1)S(1)}, bf16[3,2,16,1024]{3,2,1,0:T(8,128)(2,1)S(1)}, u32[]{:S(2)}, u32[]{:S(2)}) collective-permute-start(bf16[3,2,16,1024]{3,2,1,0:T(8,128)(2,1)S(1)} %get-tuple-element.365), channel_id=1, source_target_pairs={{2,0},{4,2},{6,4},{8,6},{10,8},{12,10},{14,12},{16,14},{18,16},{20... | collective-permute-start | bytes 589832 | tf_op jit(solution)/shard_map/while/body/eval_jaxpr/ppermute | solution.py:19
  404.4 1.9 collective-permute-start.1
  410.7 8.2 %gather_fusion = bf16[80,3,128,256]{3,2,1,0:T(8,128)(2,1)} fusion(bf16[3,8,128,256]{3,2,1,0:T(8,128)(2,1)S(1)} %dynamic-slice_bitcast_fusion.2, s32[1024]{0:T(1024)S(1)} %pad_clamp_fusion.4), kind=kCustom, calls=%fused_computation.1.clone.1 | custom fusion | bytes 31457600 | tf_op jit(solution)/shard_map/while/body/eval_jaxpr/jit(_take)/gather | solution.py:74
  420.6 2.4 gather_fusion.1
  423.0 8.0 %fusion.30 = f32[8,3,2,16,256]{4,3,2,1,0:T(8,128)S(1)} fusion(bf16[8,10,3,128,256]{4,3,2,1,0:T(8,128)(2,1)} %bitcast.98, pred[8,10]{1,0:T(8,128)(4,1)S(1)} %copy-done.5, bf16[8,10,3,2,16,128]{5,4,3,2,1,0:T(8,128)(2,1)} %bitcast.99, pred[8,10]{1,0:T(8,128)(4,1)S(1)} %copy-done.6, bf16[8,10]{1,0:T(8,128)(2,1)S(1)} %fusion.29), kind=kOutput, calls=%fused_computation.8.clone.1 | convolution fusion | flops 513146880 | bytes 18481472 | tf_op jit(solution)/shard_map/while/body/eval_jaxpr/fsarkt,frktc->rfsac/dot_general | solution.py:75
  433.6 10.9 %all_to_all.10 = f32[8,1,1024]{2,1,0:T(1,128)S(1)} all-to-all(f32[8,1,1024]{2,1,0:T(1,128)S(1)} %reshape.218), channel_id=1, replica_groups=mesh['depth'=8,'lat'=32,'freq'=2] {'depth'}, dimensions={0} | all-to-all | bytes 65536 | tf_op jit(solution)/shard_map/all_to_all | solution.py:58
  444.5 8.4 %psum.7 = f32[1024]{0:T(1024)S(1)} all-reduce(f32[1024]{0:T(1024)S(1)} %reduce_sum.20), channel_id=1, replica_groups=mesh['depth'=8,'lat'=32,'freq'=2] {'freq'}, use_global_device_ids=true, to_apply=%region_4.5 | all-reduce | flops 1024 | bytes 8192 | tf_op jit(solution)/shard_map/psum | solution.py:119
  (247 shorter events, 65.6 us)
Async XLA Ops:
  6.5 32.0 %copy-start = (bf16[3,2,128,1024]{3,2,1,0:T(8,128)(2,1)S(1)}, bf16[3,2,128,1024]{3,2,1,0:T(8,128)(2,1)}, u32[]{:S(2)}) copy-start(bf16[3,2,128,1024]{3,2,1,0:T(8,128)(2,1)} %param.8) | copy-start | bytes 4718596
  6.5 144.3 %all-gather.2.cloned.1.call-start = ((), (), s32[]{:S(2)}) async-start(), calls=%async_computation.2 | async-start | bytes 14155776 | tf_op jit(solution)/shard_map/all_gather | solution.py:97
  8.6 30.8 %all-to-all-start = ((f32[8,1,1024]{2,1,0:T(1,128)}), f32[8,1,1024]{2,1,0:T(1,128)S(1)}, u32[]{:S(2)}, u32[]{:S(2)}) async-start(f32[8,1,1024]{2,1,0:T(1,128)} %broadcast_in_dim.88), calls=%async_computation | async-start | bytes 65536 | tf_op jit(solution)/shard_map/all_to_all | solution.py:37
  150.9 10.4 %copy-start.1 = (s32[8,8,10]{2,1,0:T(8,128)}, s32[8,8,10]{2,1,0:T(8,128)S(1)}, u32[]{:S(2)}) copy-start(s32[8,8,10]{2,1,0:T(8,128)S(1)} %get-tuple-element.381) | copy-start | bytes 7684 | tf_op jit(solution)/shard_map/while
  150.9 10.4 %copy-start.3 = (s32[8,8,10]{2,1,0:T(8,128)}, s32[8,8,10]{2,1,0:T(8,128)S(1)}, u32[]{:S(2)}) copy-start(s32[8,8,10]{2,1,0:T(8,128)S(1)} %get-tuple-element.378) | copy-start | bytes 7684 | tf_op jit(solution)/shard_map/while
  150.9 22.9 %collective-permute-start = (bf16[3,2,16,1024]{3,2,1,0:T(8,128)(2,1)S(1)}, bf16[3,2,16,1024]{3,2,1,0:T(8,128)(2,1)S(1)}, u32[]{:S(2)}, u32[]{:S(2)}) collective-permute-start(bf16[3,2,16,1024]{3,2,1,0:T(8,128)(2,1)S(1)} %get-tuple-element.365), channel_id=1, source_target_pairs={{2,0},{4,2},{6,4},{8,6},{10,8},{12,10},{14,12},{16,14},{18,16},{20... | collective-permute-start | bytes 589832 | tf_op jit(solution)/shard_map/while/body/eval_jaxpr/ppermute | solution.py:19
  158.7 15.1 %collective-permute-start.1 = (bf16[3,2,16,1024]{3,2,1,0:T(8,128)(2,1)S(1)}, bf16[3,2,16,1024]{3,2,1,0:T(8,128)(2,1)}, u32[]{:S(2)}, u32[]{:S(2)}) collective-permute-start(bf16[3,2,16,1024]{3,2,1,0:T(8,128)(2,1)S(1)} %get-tuple-element.365), channel_id=1, source_target_pairs={{0,2},{2,4},{4,6},{6,8},{8,10},{10,12},{12,14},{14,16},{16,18},{18... | collective-permute-start | bytes 589832 | tf_op jit(solution)/shard_map/while/body/eval_jaxpr/ppermute | solution.py:16
  174.8 2.4 copy-start.5
  174.8 2.4 copy-start.6
  187.0 9.4 %copy-start.1 = (s32[8,8,10]{2,1,0:T(8,128)}, s32[8,8,10]{2,1,0:T(8,128)S(1)}, u32[]{:S(2)}) copy-start(s32[8,8,10]{2,1,0:T(8,128)S(1)} %get-tuple-element.381) | copy-start | bytes 7684 | tf_op jit(solution)/shard_map/while
  187.0 9.4 %copy-start.3 = (s32[8,8,10]{2,1,0:T(8,128)}, s32[8,8,10]{2,1,0:T(8,128)S(1)}, u32[]{:S(2)}) copy-start(s32[8,8,10]{2,1,0:T(8,128)S(1)} %get-tuple-element.378) | copy-start | bytes 7684 | tf_op jit(solution)/shard_map/while
  187.1 21.9 %collective-permute-start = (bf16[3,2,16,1024]{3,2,1,0:T(8,128)(2,1)S(1)}, bf16[3,2,16,1024]{3,2,1,0:T(8,128)(2,1)S(1)}, u32[]{:S(2)}, u32[]{:S(2)}) collective-permute-start(bf16[3,2,16,1024]{3,2,1,0:T(8,128)(2,1)S(1)} %get-tuple-element.365), channel_id=1, source_target_pairs={{2,0},{4,2},{6,4},{8,6},{10,8},{12,10},{14,12},{16,14},{18,16},{20... | collective-permute-start | bytes 589832 | tf_op jit(solution)/shard_map/while/body/eval_jaxpr/ppermute | solution.py:19
  193.8 15.2 %collective-permute-start.1 = (bf16[3,2,16,1024]{3,2,1,0:T(8,128)(2,1)S(1)}, bf16[3,2,16,1024]{3,2,1,0:T(8,128)(2,1)}, u32[]{:S(2)}, u32[]{:S(2)}) collective-permute-start(bf16[3,2,16,1024]{3,2,1,0:T(8,128)(2,1)S(1)} %get-tuple-element.365), channel_id=1, source_target_pairs={{0,2},{2,4},{4,6},{6,8},{8,10},{10,12},{12,14},{14,16},{16,18},{18... | collective-permute-start | bytes 589832 | tf_op jit(solution)/shard_map/while/body/eval_jaxpr/ppermute | solution.py:16
  210.0 2.4 copy-start.5
  210.0 2.4 copy-start.6
  222.2 9.3 %copy-start.1 = (s32[8,8,10]{2,1,0:T(8,128)}, s32[8,8,10]{2,1,0:T(8,128)S(1)}, u32[]{:S(2)}) copy-start(s32[8,8,10]{2,1,0:T(8,128)S(1)} %get-tuple-element.381) | copy-start | bytes 7684 | tf_op jit(solution)/shard_map/while
  222.2 9.3 %copy-start.3 = (s32[8,8,10]{2,1,0:T(8,128)}, s32[8,8,10]{2,1,0:T(8,128)S(1)}, u32[]{:S(2)}) copy-start(s32[8,8,10]{2,1,0:T(8,128)S(1)} %get-tuple-element.378) | copy-start | bytes 7684 | tf_op jit(solution)/shard_map/while
  222.2 21.8 %collective-permute-start = (bf16[3,2,16,1024]{3,2,1,0:T(8,128)(2,1)S(1)}, bf16[3,2,16,1024]{3,2,1,0:T(8,128)(2,1)S(1)}, u32[]{:S(2)}, u32[]{:S(2)}) collective-permute-start(bf16[3,2,16,1024]{3,2,1,0:T(8,128)(2,1)S(1)} %get-tuple-element.365), channel_id=1, source_target_pairs={{2,0},{4,2},{6,4},{8,6},{10,8},{12,10},{14,12},{16,14},{18,16},{20... | collective-permute-start | bytes 589832 | tf_op jit(solution)/shard_map/while/body/eval_jaxpr/ppermute | solution.py:19
  228.9 15.1 %collective-permute-start.1 = (bf16[3,2,16,1024]{3,2,1,0:T(8,128)(2,1)S(1)}, bf16[3,2,16,1024]{3,2,1,0:T(8,128)(2,1)}, u32[]{:S(2)}, u32[]{:S(2)}) collective-permute-start(bf16[3,2,16,1024]{3,2,1,0:T(8,128)(2,1)S(1)} %get-tuple-element.365), channel_id=1, source_target_pairs={{0,2},{2,4},{4,6},{6,8},{8,10},{10,12},{12,14},{14,16},{16,18},{18... | collective-permute-start | bytes 589832 | tf_op jit(solution)/shard_map/while/body/eval_jaxpr/ppermute | solution.py:16
  245.0 2.4 copy-start.5
  245.1 2.4 copy-start.6
  257.3 9.4 %copy-start.1 = (s32[8,8,10]{2,1,0:T(8,128)}, s32[8,8,10]{2,1,0:T(8,128)S(1)}, u32[]{:S(2)}) copy-start(s32[8,8,10]{2,1,0:T(8,128)S(1)} %get-tuple-element.381) | copy-start | bytes 7684 | tf_op jit(solution)/shard_map/while
  257.3 9.4 %copy-start.3 = (s32[8,8,10]{2,1,0:T(8,128)}, s32[8,8,10]{2,1,0:T(8,128)S(1)}, u32[]{:S(2)}) copy-start(s32[8,8,10]{2,1,0:T(8,128)S(1)} %get-tuple-element.378) | copy-start | bytes 7684 | tf_op jit(solution)/shard_map/while
  257.3 21.9 %collective-permute-start = (bf16[3,2,16,1024]{3,2,1,0:T(8,128)(2,1)S(1)}, bf16[3,2,16,1024]{3,2,1,0:T(8,128)(2,1)S(1)}, u32[]{:S(2)}, u32[]{:S(2)}) collective-permute-start(bf16[3,2,16,1024]{3,2,1,0:T(8,128)(2,1)S(1)} %get-tuple-element.365), channel_id=1, source_target_pairs={{2,0},{4,2},{6,4},{8,6},{10,8},{12,10},{14,12},{16,14},{18,16},{20... | collective-permute-start | bytes 589832 | tf_op jit(solution)/shard_map/while/body/eval_jaxpr/ppermute | solution.py:19
  264.0 15.2 %collective-permute-start.1 = (bf16[3,2,16,1024]{3,2,1,0:T(8,128)(2,1)S(1)}, bf16[3,2,16,1024]{3,2,1,0:T(8,128)(2,1)}, u32[]{:S(2)}, u32[]{:S(2)}) collective-permute-start(bf16[3,2,16,1024]{3,2,1,0:T(8,128)(2,1)S(1)} %get-tuple-element.365), channel_id=1, source_target_pairs={{0,2},{2,4},{4,6},{6,8},{8,10},{10,12},{12,14},{14,16},{16,18},{18... | collective-permute-start | bytes 589832 | tf_op jit(solution)/shard_map/while/body/eval_jaxpr/ppermute | solution.py:16
  280.2 2.4 copy-start.5
  292.4 9.3 %copy-start.1 = (s32[8,8,10]{2,1,0:T(8,128)}, s32[8,8,10]{2,1,0:T(8,128)S(1)}, u32[]{:S(2)}) copy-start(s32[8,8,10]{2,1,0:T(8,128)S(1)} %get-tuple-element.381) | copy-start | bytes 7684 | tf_op jit(solution)/shard_map/while
  292.4 9.3 %copy-start.3 = (s32[8,8,10]{2,1,0:T(8,128)}, s32[8,8,10]{2,1,0:T(8,128)S(1)}, u32[]{:S(2)}) copy-start(s32[8,8,10]{2,1,0:T(8,128)S(1)} %get-tuple-element.378) | copy-start | bytes 7684 | tf_op jit(solution)/shard_map/while
  292.4 21.8 %collective-permute-start = (bf16[3,2,16,1024]{3,2,1,0:T(8,128)(2,1)S(1)}, bf16[3,2,16,1024]{3,2,1,0:T(8,128)(2,1)S(1)}, u32[]{:S(2)}, u32[]{:S(2)}) collective-permute-start(bf16[3,2,16,1024]{3,2,1,0:T(8,128)(2,1)S(1)} %get-tuple-element.365), channel_id=1, source_target_pairs={{2,0},{4,2},{6,4},{8,6},{10,8},{12,10},{14,12},{16,14},{18,16},{20... | collective-permute-start | bytes 589832 | tf_op jit(solution)/shard_map/while/body/eval_jaxpr/ppermute | solution.py:19
  299.1 15.1 %collective-permute-start.1 = (bf16[3,2,16,1024]{3,2,1,0:T(8,128)(2,1)S(1)}, bf16[3,2,16,1024]{3,2,1,0:T(8,128)(2,1)}, u32[]{:S(2)}, u32[]{:S(2)}) collective-permute-start(bf16[3,2,16,1024]{3,2,1,0:T(8,128)(2,1)S(1)} %get-tuple-element.365), channel_id=1, source_target_pairs={{0,2},{2,4},{4,6},{6,8},{8,10},{10,12},{12,14},{14,16},{16,18},{18... | collective-permute-start | bytes 589832 | tf_op jit(solution)/shard_map/while/body/eval_jaxpr/ppermute | solution.py:16
  315.3 2.4 copy-start.5
  315.3 2.4 copy-start.6
  327.5 9.4 %copy-start.1 = (s32[8,8,10]{2,1,0:T(8,128)}, s32[8,8,10]{2,1,0:T(8,128)S(1)}, u32[]{:S(2)}) copy-start(s32[8,8,10]{2,1,0:T(8,128)S(1)} %get-tuple-element.381) | copy-start | bytes 7684 | tf_op jit(solution)/shard_map/while
  327.5 9.4 %copy-start.3 = (s32[8,8,10]{2,1,0:T(8,128)}, s32[8,8,10]{2,1,0:T(8,128)S(1)}, u32[]{:S(2)}) copy-start(s32[8,8,10]{2,1,0:T(8,128)S(1)} %get-tuple-element.378) | copy-start | bytes 7684 | tf_op jit(solution)/shard_map/while
  327.5 21.9 %collective-permute-start = (bf16[3,2,16,1024]{3,2,1,0:T(8,128)(2,1)S(1)}, bf16[3,2,16,1024]{3,2,1,0:T(8,128)(2,1)S(1)}, u32[]{:S(2)}, u32[]{:S(2)}) collective-permute-start(bf16[3,2,16,1024]{3,2,1,0:T(8,128)(2,1)S(1)} %get-tuple-element.365), channel_id=1, source_target_pairs={{2,0},{4,2},{6,4},{8,6},{10,8},{12,10},{14,12},{16,14},{18,16},{20... | collective-permute-start | bytes 589832 | tf_op jit(solution)/shard_map/while/body/eval_jaxpr/ppermute | solution.py:19
  334.2 15.2 %collective-permute-start.1 = (bf16[3,2,16,1024]{3,2,1,0:T(8,128)(2,1)S(1)}, bf16[3,2,16,1024]{3,2,1,0:T(8,128)(2,1)}, u32[]{:S(2)}, u32[]{:S(2)}) collective-permute-start(bf16[3,2,16,1024]{3,2,1,0:T(8,128)(2,1)S(1)} %get-tuple-element.365), channel_id=1, source_target_pairs={{0,2},{2,4},{4,6},{6,8},{8,10},{10,12},{12,14},{14,16},{16,18},{18... | collective-permute-start | bytes 589832 | tf_op jit(solution)/shard_map/while/body/eval_jaxpr/ppermute | solution.py:16
  350.5 2.4 copy-start.5
  362.7 9.3 %copy-start.1 = (s32[8,8,10]{2,1,0:T(8,128)}, s32[8,8,10]{2,1,0:T(8,128)S(1)}, u32[]{:S(2)}) copy-start(s32[8,8,10]{2,1,0:T(8,128)S(1)} %get-tuple-element.381) | copy-start | bytes 7684 | tf_op jit(solution)/shard_map/while
  362.7 9.3 %copy-start.3 = (s32[8,8,10]{2,1,0:T(8,128)}, s32[8,8,10]{2,1,0:T(8,128)S(1)}, u32[]{:S(2)}) copy-start(s32[8,8,10]{2,1,0:T(8,128)S(1)} %get-tuple-element.378) | copy-start | bytes 7684 | tf_op jit(solution)/shard_map/while
  362.7 21.8 %collective-permute-start = (bf16[3,2,16,1024]{3,2,1,0:T(8,128)(2,1)S(1)}, bf16[3,2,16,1024]{3,2,1,0:T(8,128)(2,1)S(1)}, u32[]{:S(2)}, u32[]{:S(2)}) collective-permute-start(bf16[3,2,16,1024]{3,2,1,0:T(8,128)(2,1)S(1)} %get-tuple-element.365), channel_id=1, source_target_pairs={{2,0},{4,2},{6,4},{8,6},{10,8},{12,10},{14,12},{16,14},{18,16},{20... | collective-permute-start | bytes 589832 | tf_op jit(solution)/shard_map/while/body/eval_jaxpr/ppermute | solution.py:19
  369.3 15.2 %collective-permute-start.1 = (bf16[3,2,16,1024]{3,2,1,0:T(8,128)(2,1)S(1)}, bf16[3,2,16,1024]{3,2,1,0:T(8,128)(2,1)}, u32[]{:S(2)}, u32[]{:S(2)}) collective-permute-start(bf16[3,2,16,1024]{3,2,1,0:T(8,128)(2,1)S(1)} %get-tuple-element.365), channel_id=1, source_target_pairs={{0,2},{2,4},{4,6},{6,8},{8,10},{10,12},{12,14},{14,16},{16,18},{18... | collective-permute-start | bytes 589832 | tf_op jit(solution)/shard_map/while/body/eval_jaxpr/ppermute | solution.py:16
  385.5 2.4 copy-start.5
  385.5 2.4 copy-start.6
  397.7 9.3 %copy-start.1 = (s32[8,8,10]{2,1,0:T(8,128)}, s32[8,8,10]{2,1,0:T(8,128)S(1)}, u32[]{:S(2)}) copy-start(s32[8,8,10]{2,1,0:T(8,128)S(1)} %get-tuple-element.381) | copy-start | bytes 7684 | tf_op jit(solution)/shard_map/while
  397.7 9.4 %copy-start.3 = (s32[8,8,10]{2,1,0:T(8,128)}, s32[8,8,10]{2,1,0:T(8,128)S(1)}, u32[]{:S(2)}) copy-start(s32[8,8,10]{2,1,0:T(8,128)S(1)} %get-tuple-element.378) | copy-start | bytes 7684 | tf_op jit(solution)/shard_map/while
  397.7 21.8 %collective-permute-start = (bf16[3,2,16,1024]{3,2,1,0:T(8,128)(2,1)S(1)}, bf16[3,2,16,1024]{3,2,1,0:T(8,128)(2,1)S(1)}, u32[]{:S(2)}, u32[]{:S(2)}) collective-permute-start(bf16[3,2,16,1024]{3,2,1,0:T(8,128)(2,1)S(1)} %get-tuple-element.365), channel_id=1, source_target_pairs={{2,0},{4,2},{6,4},{8,6},{10,8},{12,10},{14,12},{16,14},{18,16},{20... | collective-permute-start | bytes 589832 | tf_op jit(solution)/shard_map/while/body/eval_jaxpr/ppermute | solution.py:19
  404.4 15.1 %collective-permute-start.1 = (bf16[3,2,16,1024]{3,2,1,0:T(8,128)(2,1)S(1)}, bf16[3,2,16,1024]{3,2,1,0:T(8,128)(2,1)}, u32[]{:S(2)}, u32[]{:S(2)}) collective-permute-start(bf16[3,2,16,1024]{3,2,1,0:T(8,128)(2,1)S(1)} %get-tuple-element.365), channel_id=1, source_target_pairs={{0,2},{2,4},{4,6},{6,8},{8,10},{10,12},{12,14},{14,16},{16,18},{18... | collective-permute-start | bytes 589832 | tf_op jit(solution)/shard_map/while/body/eval_jaxpr/ppermute | solution.py:16
  420.6 2.4 copy-start.5
  (19 other events, 34.8 us)
Sparse Core Ops, SparseCore 0:
  9.4 141.3 all-gather.1
where the time goes:
time: 463 us; the launch traced here: 460 us
  local copies, waits for them, and re-layouts  114 us (25%)
  waiting for transfers between devices  112 us (24%)
  starting transfers between devices  77.6 us (17%)
  matrix products  64.4 us (14%)
  blocking collectives  40.1 us (9%)
  other arithmetic  38.8 us (8%)
  between operations  13.4 us (3%)
    all_gather x1, waiting for transfers between devices, per_device(): pool_all = lax.all_gather(pool, 'depth', axis=0, tiled=True)  111 us
    gather x8, local copies, waits for them, and re-layouts, extrapolate(): chosen = jnp.take(pool_level, block_level, axis=1)  65.3 us
    dot_general x8, matrix products, extrapolate(): jnp.einsum('fsarkt,frktc->rfsac', picked, chosen, preferred_element_type=...  64.4 us
    ppermute x8, starting transfers between devices, extended_2(): lax.ppermute(lax.slice_in_dim(block, 0, width, axis=dim), axis, backward)  54.6 us
    all_gather x1, blocking collectives, in_one_piece(): lax.all_gather(both, axis, axis=dim, tiled=True)  20.8 us
    gather x8, local copies, waits for them, and re-layouts, extrapolate(): jnp.take(tile_grid, local_ids, axis=3)  19.3 us
    ppermute x8, starting transfers between devices, extended_2(): lax.ppermute(lax.slice_in_dim(block, block.shape[dim] - width, None, axis...  15.4 us
    squeeze x8, local copies, waits for them, and re-layouts, level_step(): lax.dynamic_index_in_dim(pool_all, level_index, 0, keepdims=False)  12.1 us
  transfers between devices with their start and end apart: 18, of which 1 were waited for; matrix products, arithmetic and copies ran while one was open for 24% of the time, Pallas kernels for 0%

commit v1 on v0

--- a/solution.py
+++ b/solution.py
@@ -94,7 +94,25 @@
     lateral_width = surface.shape[3]
     shot_rows = shot_total // lax.axis_size("depth")
     own_shots = lax.dynamic_slice_in_dim(surface, depth_index * shot_rows, shot_rows, 2)
-    pool_all = lax.all_gather(pool, "depth", axis=0, tiled=True)
+    y_new = jax.lax.axis_size("depth")
+    next_value = jax.lax.axis_index("depth")
+    right_arr, z, extra = (y_new, next_value, pool.shape[0])
+    tray = [(p, (p + 1) % right_arr) for p in range(right_arr)]
+    line_up = [(p, (p - 1) % right_arr) for p in range(right_arr)]
+    pool_all = jnp.zeros((*pool.shape[:0], right_arr * extra, *pool.shape[1:]), pool.dtype)
+    pool_all = lax.dynamic_update_slice_in_dim(pool_all, pool, z * extra, axis=0)
+    tile_out = arr_next = pool
+    long_array = right_arr // 2
+    for idx in tuple(range(1, long_array + 1)):
+        tile_out = jax.lax.ppermute(tile_out, "depth", tray)
+        pool_all = lax.dynamic_update_slice_in_dim(
+            pool_all, tile_out, (z - idx) % right_arr * extra, axis=0
+        )
+        if idx < right_arr - long_array:
+            arr_next = jax.lax.ppermute(arr_next, "depth", line_up)
+            pool_all = lax.dynamic_update_slice_in_dim(
+                pool_all, arr_next, (z + idx) % right_arr * extra, axis=0
+            )
     ids_all, blocks_all, counts_all = in_one_piece((tile_ids, block_ids, counts), "depth", 0, 2)
     refl_all = gather_directly(refl, "depth", 0)
     level_total = pool_all.shape[0]

time: 463 us -> 521 us (1.13)
  starting transfers between devices: 77.6 us -> 112 us
  blocking collectives: 40.1 us -> 69.1 us
  waiting for transfers between devices: 112 us -> 86.3 us
  local copies, waits for them, and re-layouts: 114 us -> 136 us
  between operations: 13.4 us -> 0.22 us
  other arithmetic: 38.8 us -> 49.2 us
    all_gather x1 -> x0, waiting for transfers between devices: 111 us -> none  [per_device(): pool_all = lax.all_gather(pool, 'depth', axis=0, tiled=True)]
    ppermute x0 -> x7, waiting for transfers between devices: none -> 86.2 us  [the longest x4 85.9 us: per_device(): tile_out = jax.lax.ppermute(tile_out, 'depth', tray)]
    ppermute x0 -> x7, starting transfers between devices: none -> 26.6 us  [the longest x4 14.4 us: per_device(): tile_out = jax.lax.ppermute(tile_out, 'depth', tray)]
    all_gather x1, blocking collectives: 20.8 us -> 40.1 us  [in_one_piece(): lax.all_gather(both, axis, axis=dim, tiled=True)]
    dynamic_update_slice x0 -> x8, local copies, waits for them, and re-layouts: none -> 16 us  [the longest x4 8.04 us: per_device(): lax.dynamic_update_slice_in_dim(pool_all, tile_out, (z - idx) % right_arr...]
    psum x1, blocking collectives: 8.41 us -> 17.5 us  [per_device(): summed = lax.psum(image_local, 'freq')]
    broadcast_in_dim x0 -> x1, local copies, waits for them, and re-layouts: none -> 6.24 us  [per_device(): jnp.zeros((*pool.shape[:0], right_arr * extra, *pool.shape[1:]), pool.dtype)]
    and x8, other arithmetic: 4.85 us -> 10.4 us  [extrapolate(): chosen = jnp.take(pool_level, block_level, axis=1)]
  transfers between devices with their start and end apart: 18 -> 24, of which waited for: 1 -> 4; matrix products, arithmetic and copies ran while one was open for 24% -> 27% of each run, Pallas kernels for 0% -> 0%
where the time goes in v1:
time: 521 us; the launch traced here: 518 us
  local copies, waits for them, and re-layouts  136 us (26%)
  starting transfers between devices  112 us (21%)
  waiting for transfers between devices  86.3 us (17%)
  blocking collectives  69.1 us (13%)
  matrix products  64.4 us (12%)
  other arithmetic  49.2 us (9%)
    ppermute x4, waiting for transfers between devices, per_device(): tile_out = jax.lax.ppermute(tile_out, 'depth', tray)  85.9 us
    gather x8, local copies, waits for them, and re-layouts, extrapolate(): chosen = jnp.take(pool_level, block_level, axis=1)  65.2 us
    dot_general x8, matrix products, extrapolate(): jnp.einsum('fsarkt,frktc->rfsac', picked, chosen, preferred_element_type=...  64.4 us
    ppermute x8, starting transfers between devices, extended_2(): lax.ppermute(lax.slice_in_dim(block, 0, width, axis=dim), axis, backward)  59.9 us
    all_gather x1, blocking collectives, in_one_piece(): lax.all_gather(both, axis, axis=dim, tiled=True)  40.1 us
    gather x8, local copies, waits for them, and re-layouts, extrapolate(): jnp.take(tile_grid, local_ids, axis=3)  19.3 us
    psum x1, blocking collectives, per_device(): summed = lax.psum(image_local, 'freq')  17.5 us
    ppermute x8, starting transfers between devices, extended_2(): lax.ppermute(lax.slice_in_dim(block, block.shape[dim] - width, None, axis...  15.4 us
  transfers between devices with their start and end apart: 24, of which 4 were waited for; matrix products, arithmetic and copies ran while one was open for 27% of the time, Pallas kernels for 0%

profile of v1, /device:TPU:1, one launch (start us, length us, event | category | flops | bytes accessed | tf_op | source)
XLA Modules:
  0.0 517.6 jit_solution(12659916028505848471)
XLA Ops:
  0.0 4.2 collective-permute-start.2
  4.2 3.8 collective-permute-start.3
  8.0 27.2 %collective-permute-done.2 = bf16[1,3,8,128,256]{4,3,2,1,0:T(8,128)(2,1)S(1)} collective-permute-done((bf16[1,3,8,128,256]{4,3,2,1,0:T(8,128)(2,1)}, bf16[1,3,8,128,256]{4,3,2,1,0:T(8,128)(2,1)S(1)}, u32[]{:S(2)}, u32[]{:S(2)}) %collective-permute-start.2) | collective-permute-done | bytes 1572896 | tf_op jit(solution)/shard_map/ppermute | solution.py:107
  35.2 5.8 %collective-permute-start.4 = (bf16[1,3,8,128,256]{4,3,2,1,0:T(8,128)(2,1)S(1)}, bf16[1,3,8,128,256]{4,3,2,1,0:T(8,128)(2,1)S(1)}, u32[]{:S(2)}, u32[]{:S(2)}) collective-permute-start(bf16[1,3,8,128,256]{4,3,2,1,0:T(8,128)(2,1)S(1)} %collective-permute-done.2), channel_id=1, source_target_pairs={{0,64},{64,128},{128,192},{192,256},{256,320},{320,384},{384,448},... | collective-permute-start | bytes 4718600 | tf_op jit(solution)/shard_map/ppermute | solution.py:107
  41.0 4.3 collective-permute-start.5
  45.4 29.7 %collective-permute-done.4 = bf16[1,3,8,128,256]{4,3,2,1,0:T(8,128)(2,1)S(1)} collective-permute-done((bf16[1,3,8,128,256]{4,3,2,1,0:T(8,128)(2,1)S(1)}, bf16[1,3,8,128,256]{4,3,2,1,0:T(8,128)(2,1)S(1)}, u32[]{:S(2)}, u32[]{:S(2)}) %collective-permute-start.4) | collective-permute-done | bytes 1572896 | tf_op jit(solution)/shard_map/ppermute | solution.py:107
  77.6 4.1 collective-permute-start.7
  81.7 29.0 %collective-permute-done.6 = bf16[1,3,8,128,256]{4,3,2,1,0:T(8,128)(2,1)} collective-permute-done((bf16[1,3,8,128,256]{4,3,2,1,0:T(8,128)(2,1)S(1)}, bf16[1,3,8,128,256]{4,3,2,1,0:T(8,128)(2,1)}, u32[]{:S(2)}, u32[]{:S(2)}) %collective-permute-start.6) | collective-permute-done | bytes 1572896 | tf_op jit(solution)/shard_map/ppermute | solution.py:107
  114.2 9.7 %all-to-all-start = ((f32[8,1,1024]{2,1,0:T(1,128)}), f32[8,1,1024]{2,1,0:T(1,128)S(1)}, u32[]{:S(2)}, u32[]{:S(2)}) async-start(f32[8,1,1024]{2,1,0:T(1,128)} %broadcast_in_dim.92), calls=%async_computation | async-start | bytes 65536 | tf_op jit(solution)/shard_map/all_to_all | solution.py:37
  125.4 40.1 %all_gather.3 = s32[8,8,21]{2,1,0:T(8,128)S(1)} all-gather(s32[1,8,21]{2,1,0:T(8,128)S(1)} %pad_add_fusion), channel_id=1, replica_groups=mesh['depth'=8,'lat'=32,'freq'=2] {'depth'}, dimensions={0}, use_global_device_ids=true | all-gather | bytes 6048 | tf_op jit(solution)/shard_map/all_gather | solution.py:27
  165.6 6.2 %broadcast_in_dim.91 = bf16[8,3,8,128,256]{4,3,2,1,0:T(8,128)(2,1)} broadcast(bf16[]{:T(256)} %constant.223.clone.1), dimensions={} | broadcast | bytes 12582914 | tf_op jit(solution)/shard_map/broadcast_in_dim | solution.py:102
  179.1 2.7 constant_dynamic-update-slice_fusion.3
  181.8 2.8 constant_dynamic-update-slice_fusion.2
  184.6 2.7 constant_dynamic-update-slice_fusion.1
  187.3 2.7 constant_dynamic-update-slice_fusion
  190.1 297.1 %while.17 = (s32[]{:T(128)}, bf16[3,2,16,1024]{3,2,1,0:T(8,128)(2,1)S(1)}, f32[8,1024]{1,0:T(8,128)}, s32[8,8,10]{2,1,0:T(8,128)}, s32[]{:T(128)}, /*index=5*/s3...) while((s32[]{:T(128)}, ...), condition=%wide.region_2.3_spmd, body=%wide.region_0.2_spmd.sunk | while | flops 515904960 | bytes 61974620 | solution.py:135
  190.1 13.2 %collective-permute-start = (bf16[3,2,16,1024]{3,2,1,0:T(8,128)(2,1)S(1)}, bf16[3,2,16,1024]{3,2,1,0:T(8,128)(2,1)S(1)}, u32[]{:S(2)}, u32[]{:S(2)}) collective-permute-start(bf16[3,2,16,1024]{3,2,1,0:T(8,128)(2,1)S(1)} %get-tuple-element.365), channel_id=1, source_target_pairs={{2,0},{4,2},{6,4},{8,6},{10,8},{12,10},{14,12},{16,14},{18,16},{20... | collective-permute-start | bytes 589832 | tf_op jit(solution)/shard_map/while/body/eval_jaxpr/ppermute | solution.py:19
  210.8 8.1 %gather_fusion = bf16[80,3,128,256]{3,2,1,0:T(8,128)(2,1)} fusion(bf16[3,8,128,256]{3,2,1,0:T(8,128)(2,1)S(1)} %dynamic-slice_bitcast_fusion.2, s32[1024]{0:T(1024)S(1)} %pad_clamp_fusion.4), kind=kCustom, calls=%fused_computation.1.clone.1 | custom fusion | bytes 31457600 | tf_op jit(solution)/shard_map/while/body/eval_jaxpr/jit(_take)/gather | solution.py:74
  220.7 2.4 gather_fusion.1
  223.1 8.0 %fusion.30 = f32[8,3,2,16,256]{4,3,2,1,0:T(8,128)S(1)} fusion(bf16[8,10,3,128,256]{4,3,2,1,0:T(8,128)(2,1)} %bitcast.98, pred[8,10]{1,0:T(8,128)(4,1)S(1)} %copy-done.6, bf16[8,10,3,2,16,128]{5,4,3,2,1,0:T(8,128)(2,1)} %bitcast.99, pred[8,10]{1,0:T(8,128)(4,1)S(1)} %copy-done.7, bf16[8,10]{1,0:T(8,128)(2,1)S(1)} %fusion.29), kind=kOutput, calls=%fused_computation.8.clone.1 | convolution fusion | flops 513146880 | bytes 18481472 | tf_op jit(solution)/shard_map/while/body/eval_jaxpr/fsarkt,frktc->rfsac/dot_general | solution.py:75
  232.9 6.7 %collective-permute-start = (bf16[3,2,16,1024]{3,2,1,0:T(8,128)(2,1)S(1)}, bf16[3,2,16,1024]{3,2,1,0:T(8,128)(2,1)S(1)}, u32[]{:S(2)}, u32[]{:S(2)}) collective-permute-start(bf16[3,2,16,1024]{3,2,1,0:T(8,128)(2,1)S(1)} %get-tuple-element.365), channel_id=1, source_target_pairs={{2,0},{4,2},{6,4},{8,6},{10,8},{12,10},{14,12},{16,14},{18,16},{20... | collective-permute-start | bytes 589832 | tf_op jit(solution)/shard_map/while/body/eval_jaxpr/ppermute | solution.py:19
  247.2 8.2 %gather_fusion = bf16[80,3,128,256]{3,2,1,0:T(8,128)(2,1)} fusion(bf16[3,8,128,256]{3,2,1,0:T(8,128)(2,1)S(1)} %dynamic-slice_bitcast_fusion.2, s32[1024]{0:T(1024)S(1)} %pad_clamp_fusion.4), kind=kCustom, calls=%fused_computation.1.clone.1 | custom fusion | bytes 31457600 | tf_op jit(solution)/shard_map/while/body/eval_jaxpr/jit(_take)/gather | solution.py:74
  257.1 2.4 gather_fusion.1
  259.5 8.0 %fusion.30 = f32[8,3,2,16,256]{4,3,2,1,0:T(8,128)S(1)} fusion(bf16[8,10,3,128,256]{4,3,2,1,0:T(8,128)(2,1)} %bitcast.98, pred[8,10]{1,0:T(8,128)(4,1)S(1)} %copy-done.6, bf16[8,10,3,2,16,128]{5,4,3,2,1,0:T(8,128)(2,1)} %bitcast.99, pred[8,10]{1,0:T(8,128)(4,1)S(1)} %copy-done.7, bf16[8,10]{1,0:T(8,128)(2,1)S(1)} %fusion.29), kind=kOutput, calls=%fused_computation.8.clone.1 | convolution fusion | flops 513146880 | bytes 18481472 | tf_op jit(solution)/shard_map/while/body/eval_jaxpr/fsarkt,frktc->rfsac/dot_general | solution.py:75
  269.2 6.7 %collective-permute-start = (bf16[3,2,16,1024]{3,2,1,0:T(8,128)(2,1)S(1)}, bf16[3,2,16,1024]{3,2,1,0:T(8,128)(2,1)S(1)}, u32[]{:S(2)}, u32[]{:S(2)}) collective-permute-start(bf16[3,2,16,1024]{3,2,1,0:T(8,128)(2,1)S(1)} %get-tuple-element.365), channel_id=1, source_target_pairs={{2,0},{4,2},{6,4},{8,6},{10,8},{12,10},{14,12},{16,14},{18,16},{20... | collective-permute-start | bytes 589832 | tf_op jit(solution)/shard_map/while/body/eval_jaxpr/ppermute | solution.py:19
  283.5 8.1 %gather_fusion = bf16[80,3,128,256]{3,2,1,0:T(8,128)(2,1)} fusion(bf16[3,8,128,256]{3,2,1,0:T(8,128)(2,1)S(1)} %dynamic-slice_bitcast_fusion.2, s32[1024]{0:T(1024)S(1)} %pad_clamp_fusion.4), kind=kCustom, calls=%fused_computation.1.clone.1 | custom fusion | bytes 31457600 | tf_op jit(solution)/shard_map/while/body/eval_jaxpr/jit(_take)/gather | solution.py:74
  293.4 2.4 gather_fusion.1
  295.8 8.0 %fusion.30 = f32[8,3,2,16,256]{4,3,2,1,0:T(8,128)S(1)} fusion(bf16[8,10,3,128,256]{4,3,2,1,0:T(8,128)(2,1)} %bitcast.98, pred[8,10]{1,0:T(8,128)(4,1)S(1)} %copy-done.6, bf16[8,10,3,2,16,128]{5,4,3,2,1,0:T(8,128)(2,1)} %bitcast.99, pred[8,10]{1,0:T(8,128)(4,1)S(1)} %copy-done.7, bf16[8,10]{1,0:T(8,128)(2,1)S(1)} %fusion.29), kind=kOutput, calls=%fused_computation.8.clone.1 | convolution fusion | flops 513146880 | bytes 18481472 | tf_op jit(solution)/shard_map/while/body/eval_jaxpr/fsarkt,frktc->rfsac/dot_general | solution.py:75
  305.5 6.7 %collective-permute-start = (bf16[3,2,16,1024]{3,2,1,0:T(8,128)(2,1)S(1)}, bf16[3,2,16,1024]{3,2,1,0:T(8,128)(2,1)S(1)}, u32[]{:S(2)}, u32[]{:S(2)}) collective-permute-start(bf16[3,2,16,1024]{3,2,1,0:T(8,128)(2,1)S(1)} %get-tuple-element.365), channel_id=1, source_target_pairs={{2,0},{4,2},{6,4},{8,6},{10,8},{12,10},{14,12},{16,14},{18,16},{20... | collective-permute-start | bytes 589832 | tf_op jit(solution)/shard_map/while/body/eval_jaxpr/ppermute | solution.py:19
  319.9 8.2 %gather_fusion = bf16[80,3,128,256]{3,2,1,0:T(8,128)(2,1)} fusion(bf16[3,8,128,256]{3,2,1,0:T(8,128)(2,1)S(1)} %dynamic-slice_bitcast_fusion.2, s32[1024]{0:T(1024)S(1)} %pad_clamp_fusion.4), kind=kCustom, calls=%fused_computation.1.clone.1 | custom fusion | bytes 31457600 | tf_op jit(solution)/shard_map/while/body/eval_jaxpr/jit(_take)/gather | solution.py:74
  329.8 2.4 gather_fusion.1
  332.2 8.0 %fusion.30 = f32[8,3,2,16,256]{4,3,2,1,0:T(8,128)S(1)} fusion(bf16[8,10,3,128,256]{4,3,2,1,0:T(8,128)(2,1)} %bitcast.98, pred[8,10]{1,0:T(8,128)(4,1)S(1)} %copy-done.6, bf16[8,10,3,2,16,128]{5,4,3,2,1,0:T(8,128)(2,1)} %bitcast.99, pred[8,10]{1,0:T(8,128)(4,1)S(1)} %copy-done.7, bf16[8,10]{1,0:T(8,128)(2,1)S(1)} %fusion.29), kind=kOutput, calls=%fused_computation.8.clone.1 | convolution fusion | flops 513146880 | bytes 18481472 | tf_op jit(solution)/shard_map/while/body/eval_jaxpr/fsarkt,frktc->rfsac/dot_general | solution.py:75
  342.0 6.7 %collective-permute-start = (bf16[3,2,16,1024]{3,2,1,0:T(8,128)(2,1)S(1)}, bf16[3,2,16,1024]{3,2,1,0:T(8,128)(2,1)S(1)}, u32[]{:S(2)}, u32[]{:S(2)}) collective-permute-start(bf16[3,2,16,1024]{3,2,1,0:T(8,128)(2,1)S(1)} %get-tuple-element.365), channel_id=1, source_target_pairs={{2,0},{4,2},{6,4},{8,6},{10,8},{12,10},{14,12},{16,14},{18,16},{20... | collective-permute-start | bytes 589832 | tf_op jit(solution)/shard_map/while/body/eval_jaxpr/ppermute | solution.py:19
  356.2 8.1 %gather_fusion = bf16[80,3,128,256]{3,2,1,0:T(8,128)(2,1)} fusion(bf16[3,8,128,256]{3,2,1,0:T(8,128)(2,1)S(1)} %dynamic-slice_bitcast_fusion.2, s32[1024]{0:T(1024)S(1)} %pad_clamp_fusion.4), kind=kCustom, calls=%fused_computation.1.clone.1 | custom fusion | bytes 31457600 | tf_op jit(solution)/shard_map/while/body/eval_jaxpr/jit(_take)/gather | solution.py:74
  366.1 2.4 gather_fusion.1
  368.5 8.0 %fusion.30 = f32[8,3,2,16,256]{4,3,2,1,0:T(8,128)S(1)} fusion(bf16[8,10,3,128,256]{4,3,2,1,0:T(8,128)(2,1)} %bitcast.98, pred[8,10]{1,0:T(8,128)(4,1)S(1)} %copy-done.6, bf16[8,10,3,2,16,128]{5,4,3,2,1,0:T(8,128)(2,1)} %bitcast.99, pred[8,10]{1,0:T(8,128)(4,1)S(1)} %copy-done.7, bf16[8,10]{1,0:T(8,128)(2,1)S(1)} %fusion.29), kind=kOutput, calls=%fused_computation.8.clone.1 | convolution fusion | flops 513146880 | bytes 18481472 | tf_op jit(solution)/shard_map/while/body/eval_jaxpr/fsarkt,frktc->rfsac/dot_general | solution.py:75
  378.2 6.7 %collective-permute-start = (bf16[3,2,16,1024]{3,2,1,0:T(8,128)(2,1)S(1)}, bf16[3,2,16,1024]{3,2,1,0:T(8,128)(2,1)S(1)}, u32[]{:S(2)}, u32[]{:S(2)}) collective-permute-start(bf16[3,2,16,1024]{3,2,1,0:T(8,128)(2,1)S(1)} %get-tuple-element.365), channel_id=1, source_target_pairs={{2,0},{4,2},{6,4},{8,6},{10,8},{12,10},{14,12},{16,14},{18,16},{20... | collective-permute-start | bytes 589832 | tf_op jit(solution)/shard_map/while/body/eval_jaxpr/ppermute | solution.py:19
  392.5 8.2 %gather_fusion = bf16[80,3,128,256]{3,2,1,0:T(8,128)(2,1)} fusion(bf16[3,8,128,256]{3,2,1,0:T(8,128)(2,1)S(1)} %dynamic-slice_bitcast_fusion.2, s32[1024]{0:T(1024)S(1)} %pad_clamp_fusion.4), kind=kCustom, calls=%fused_computation.1.clone.1 | custom fusion | bytes 31457600 | tf_op jit(solution)/shard_map/while/body/eval_jaxpr/jit(_take)/gather | solution.py:74
  404.9 8.0 %fusion.30 = f32[8,3,2,16,256]{4,3,2,1,0:T(8,128)S(1)} fusion(bf16[8,10,3,128,256]{4,3,2,1,0:T(8,128)(2,1)} %bitcast.98, pred[8,10]{1,0:T(8,128)(4,1)S(1)} %copy-done.6, bf16[8,10,3,2,16,128]{5,4,3,2,1,0:T(8,128)(2,1)} %bitcast.99, pred[8,10]{1,0:T(8,128)(4,1)S(1)} %copy-done.7, bf16[8,10]{1,0:T(8,128)(2,1)S(1)} %fusion.29), kind=kOutput, calls=%fused_computation.8.clone.1 | convolution fusion | flops 513146880 | bytes 18481472 | tf_op jit(solution)/shard_map/while/body/eval_jaxpr/fsarkt,frktc->rfsac/dot_general | solution.py:75
  414.6 6.6 %collective-permute-start = (bf16[3,2,16,1024]{3,2,1,0:T(8,128)(2,1)S(1)}, bf16[3,2,16,1024]{3,2,1,0:T(8,128)(2,1)S(1)}, u32[]{:S(2)}, u32[]{:S(2)}) collective-permute-start(bf16[3,2,16,1024]{3,2,1,0:T(8,128)(2,1)S(1)} %get-tuple-element.365), channel_id=1, source_target_pairs={{2,0},{4,2},{6,4},{8,6},{10,8},{12,10},{14,12},{16,14},{18,16},{20... | collective-permute-start | bytes 589832 | tf_op jit(solution)/shard_map/while/body/eval_jaxpr/ppermute | solution.py:19
  428.8 8.2 %gather_fusion = bf16[80,3,128,256]{3,2,1,0:T(8,128)(2,1)} fusion(bf16[3,8,128,256]{3,2,1,0:T(8,128)(2,1)S(1)} %dynamic-slice_bitcast_fusion.2, s32[1024]{0:T(1024)S(1)} %pad_clamp_fusion.4), kind=kCustom, calls=%fused_computation.1.clone.1 | custom fusion | bytes 31457600 | tf_op jit(solution)/shard_map/while/body/eval_jaxpr/jit(_take)/gather | solution.py:74
  438.7 2.4 gather_fusion.1
  441.1 8.0 %fusion.30 = f32[8,3,2,16,256]{4,3,2,1,0:T(8,128)S(1)} fusion(bf16[8,10,3,128,256]{4,3,2,1,0:T(8,128)(2,1)} %bitcast.98, pred[8,10]{1,0:T(8,128)(4,1)S(1)} %copy-done.6, bf16[8,10,3,2,16,128]{5,4,3,2,1,0:T(8,128)(2,1)} %bitcast.99, pred[8,10]{1,0:T(8,128)(4,1)S(1)} %copy-done.7, bf16[8,10]{1,0:T(8,128)(2,1)S(1)} %fusion.29), kind=kOutput, calls=%fused_computation.8.clone.1 | convolution fusion | flops 513146880 | bytes 18481472 | tf_op jit(solution)/shard_map/while/body/eval_jaxpr/fsarkt,frktc->rfsac/dot_general | solution.py:75
  450.9 6.7 %collective-permute-start = (bf16[3,2,16,1024]{3,2,1,0:T(8,128)(2,1)S(1)}, bf16[3,2,16,1024]{3,2,1,0:T(8,128)(2,1)S(1)}, u32[]{:S(2)}, u32[]{:S(2)}) collective-permute-start(bf16[3,2,16,1024]{3,2,1,0:T(8,128)(2,1)S(1)} %get-tuple-element.365), channel_id=1, source_target_pairs={{2,0},{4,2},{6,4},{8,6},{10,8},{12,10},{14,12},{16,14},{18,16},{20... | collective-permute-start | bytes 589832 | tf_op jit(solution)/shard_map/while/body/eval_jaxpr/ppermute | solution.py:19
  465.1 8.1 %gather_fusion = bf16[80,3,128,256]{3,2,1,0:T(8,128)(2,1)} fusion(bf16[3,8,128,256]{3,2,1,0:T(8,128)(2,1)S(1)} %dynamic-slice_bitcast_fusion.2, s32[1024]{0:T(1024)S(1)} %pad_clamp_fusion.4), kind=kCustom, calls=%fused_computation.1.clone.1 | custom fusion | bytes 31457600 | tf_op jit(solution)/shard_map/while/body/eval_jaxpr/jit(_take)/gather | solution.py:74
  477.4 8.0 %fusion.30 = f32[8,3,2,16,256]{4,3,2,1,0:T(8,128)S(1)} fusion(bf16[8,10,3,128,256]{4,3,2,1,0:T(8,128)(2,1)} %bitcast.98, pred[8,10]{1,0:T(8,128)(4,1)S(1)} %copy-done.6, bf16[8,10,3,2,16,128]{5,4,3,2,1,0:T(8,128)(2,1)} %bitcast.99, pred[8,10]{1,0:T(8,128)(4,1)S(1)} %copy-done.7, bf16[8,10]{1,0:T(8,128)(2,1)S(1)} %fusion.29), kind=kOutput, calls=%fused_computation.8.clone.1 | convolution fusion | flops 513146880 | bytes 18481472 | tf_op jit(solution)/shard_map/while/body/eval_jaxpr/fsarkt,frktc->rfsac/dot_general | solution.py:75
  488.0 11.5 %all_to_all.10 = f32[8,1,1024]{2,1,0:T(1,128)S(1)} all-to-all(f32[8,1,1024]{2,1,0:T(1,128)S(1)} %reshape.218), channel_id=1, replica_groups=mesh['depth'=8,'lat'=32,'freq'=2] {'depth'}, dimensions={0} | all-to-all | bytes 65536 | tf_op jit(solution)/shard_map/all_to_all | solution.py:58
  499.5 17.5 %psum.7 = f32[1024]{0:T(1024)S(1)} all-reduce(f32[1024]{0:T(1024)S(1)} %reduce_sum.20), channel_id=1, replica_groups=mesh['depth'=8,'lat'=32,'freq'=2] {'freq'}, use_global_device_ids=true, to_apply=%region_4.5 | all-reduce | flops 1024 | bytes 8192 | tf_op jit(solution)/shard_map/psum | solution.py:137
  (213 shorter events, 108.8 us)
Async XLA Ops:
  0.0 173.7 %copy-start = (bf16[3,2,128,1024]{3,2,1,0:T(8,128)(2,1)S(1)}, bf16[3,2,128,1024]{3,2,1,0:T(8,128)(2,1)}, u32[]{:S(2)}) copy-start(bf16[3,2,128,1024]{3,2,1,0:T(8,128)(2,1)} %param.8) | copy-start | bytes 4718596
  0.0 35.2 %collective-permute-start.2 = (bf16[1,3,8,128,256]{4,3,2,1,0:T(8,128)(2,1)}, bf16[1,3,8,128,256]{4,3,2,1,0:T(8,128)(2,1)S(1)}, u32[]{:S(2)}, u32[]{:S(2)}) collective-permute-start(bf16[1,3,8,128,256]{4,3,2,1,0:T(8,128)(2,1)} %param.10), channel_id=1, source_target_pairs={{0,64},{64,128},{128,192},{192,256},{256,320},{320,384},{384,448},... | collective-permute-start | bytes 4718600 | tf_op jit(solution)/shard_map/ppermute | solution.py:107
  4.2 36.8 %collective-permute-start.3 = (bf16[1,3,8,128,256]{4,3,2,1,0:T(8,128)(2,1)}, bf16[1,3,8,128,256]{4,3,2,1,0:T(8,128)(2,1)S(1)}, u32[]{:S(2)}, u32[]{:S(2)}) collective-permute-start(bf16[1,3,8,128,256]{4,3,2,1,0:T(8,128)(2,1)} %param.10), channel_id=1, source_target_pairs={{0,448},{64,0},{128,64},{192,128},{256,192},{320,256},{384,320},{4... | collective-permute-start | bytes 4718600 | tf_op jit(solution)/shard_map/ppermute | solution.py:112
  35.2 39.9 %collective-permute-start.4 = (bf16[1,3,8,128,256]{4,3,2,1,0:T(8,128)(2,1)S(1)}, bf16[1,3,8,128,256]{4,3,2,1,0:T(8,128)(2,1)S(1)}, u32[]{:S(2)}, u32[]{:S(2)}) collective-permute-start(bf16[1,3,8,128,256]{4,3,2,1,0:T(8,128)(2,1)S(1)} %collective-permute-done.2), channel_id=1, source_target_pairs={{0,64},{64,128},{128,192},{192,256},{256,320},{320,384},{384,448},... | collective-permute-start | bytes 4718600 | tf_op jit(solution)/shard_map/ppermute | solution.py:107
  41.0 34.1 %copy-start.2 = (bf16[1,3,8,128,256]{4,3,2,1,0:T(8,128)(2,1)}, bf16[1,3,8,128,256]{4,3,2,1,0:T(8,128)(2,1)S(1)}, u32[]{:S(2)}) copy-start(bf16[1,3,8,128,256]{4,3,2,1,0:T(8,128)(2,1)S(1)} %collective-permute-done.3) | copy-start | bytes 4718596
  41.0 36.6 %collective-permute-start.5 = (bf16[1,3,8,128,256]{4,3,2,1,0:T(8,128)(2,1)S(1)}, bf16[1,3,8,128,256]{4,3,2,1,0:T(8,128)(2,1)}, u32[]{:S(2)}, u32[]{:S(2)}) collective-permute-start(bf16[1,3,8,128,256]{4,3,2,1,0:T(8,128)(2,1)S(1)} %collective-permute-done.3), channel_id=1, source_target_pairs={{0,448},{64,0},{128,64},{192,128},{256,192},{320,256},{384,320},{4... | collective-permute-start | bytes 4718600 | tf_op jit(solution)/shard_map/ppermute | solution.py:112
  75.1 2.5 copy-start.4
  75.1 35.6 %collective-permute-start.6 = (bf16[1,3,8,128,256]{4,3,2,1,0:T(8,128)(2,1)S(1)}, bf16[1,3,8,128,256]{4,3,2,1,0:T(8,128)(2,1)}, u32[]{:S(2)}, u32[]{:S(2)}) collective-permute-start(bf16[1,3,8,128,256]{4,3,2,1,0:T(8,128)(2,1)S(1)} %collective-permute-done.4), channel_id=1, source_target_pairs={{0,64},{64,128},{128,192},{192,256},{256,320},{320,384},{384,448},... | collective-permute-start | bytes 4718600 | tf_op jit(solution)/shard_map/ppermute | solution.py:107
  77.6 107.0 %collective-permute-start.7 = (bf16[1,3,8,128,256]{4,3,2,1,0:T(8,128)(2,1)}, bf16[1,3,8,128,256]{4,3,2,1,0:T(8,128)(2,1)}, u32[]{:S(2)}, u32[]{:S(2)}) collective-permute-start(bf16[1,3,8,128,256]{4,3,2,1,0:T(8,128)(2,1)} %collective-permute-done.5), channel_id=1, source_target_pairs={{0,448},{64,0},{128,64},{192,128},{256,192},{320,256},{384,320},{4... | collective-permute-start | bytes 4718600 | tf_op jit(solution)/shard_map/ppermute | solution.py:112
  110.7 76.6 %collective-permute-start.8 = (bf16[1,3,8,128,256]{4,3,2,1,0:T(8,128)(2,1)}, bf16[1,3,8,128,256]{4,3,2,1,0:T(8,128)(2,1)}, u32[]{:S(2)}, u32[]{:S(2)}) collective-permute-start(bf16[1,3,8,128,256]{4,3,2,1,0:T(8,128)(2,1)} %collective-permute-done.6), channel_id=1, source_target_pairs={{0,64},{64,128},{128,192},{192,256},{256,320},{320,384},{384,448},... | collective-permute-start | bytes 4718600 | tf_op jit(solution)/shard_map/ppermute | solution.py:107
  114.2 60.4 %all-to-all-start = ((f32[8,1,1024]{2,1,0:T(1,128)}), f32[8,1,1024]{2,1,0:T(1,128)S(1)}, u32[]{:S(2)}, u32[]{:S(2)}) async-start(f32[8,1,1024]{2,1,0:T(1,128)} %broadcast_in_dim.92), calls=%async_computation | async-start | bytes 65536 | tf_op jit(solution)/shard_map/all_to_all | solution.py:37
  165.6 6.2 %copy-start.1 = (bf16[1,3,8,128,256]{4,3,2,1,0:T(8,128)(2,1)S(1)}, bf16[1,3,8,128,256]{4,3,2,1,0:T(8,128)(2,1)}, u32[]{:S(2)}) copy-start(bf16[1,3,8,128,256]{4,3,2,1,0:T(8,128)(2,1)} %param.10) | copy-start | bytes 4718596
  174.7 1.9 copy-start.3
  175.3 2.5 copy-start.5
  190.1 29.6 %collective-permute-start = (bf16[3,2,16,1024]{3,2,1,0:T(8,128)(2,1)S(1)}, bf16[3,2,16,1024]{3,2,1,0:T(8,128)(2,1)S(1)}, u32[]{:S(2)}, u32[]{:S(2)}) collective-permute-start(bf16[3,2,16,1024]{3,2,1,0:T(8,128)(2,1)S(1)} %get-tuple-element.365), channel_id=1, source_target_pairs={{2,0},{4,2},{6,4},{8,6},{10,8},{12,10},{14,12},{16,14},{18,16},{20... | collective-permute-start | bytes 589832 | tf_op jit(solution)/shard_map/while/body/eval_jaxpr/ppermute | solution.py:19
  203.2 16.4 %collective-permute-start.1 = (bf16[3,2,16,1024]{3,2,1,0:T(8,128)(2,1)S(1)}, bf16[3,2,16,1024]{3,2,1,0:T(8,128)(2,1)}, u32[]{:S(2)}, u32[]{:S(2)}) collective-permute-start(bf16[3,2,16,1024]{3,2,1,0:T(8,128)(2,1)S(1)} %get-tuple-element.365), channel_id=1, source_target_pairs={{0,2},{2,4},{4,6},{6,8},{8,10},{10,12},{12,14},{14,16},{16,18},{18... | collective-permute-start | bytes 589832 | tf_op jit(solution)/shard_map/while/body/eval_jaxpr/ppermute | solution.py:16
  220.7 2.4 copy-start.6
  220.7 2.4 copy-start.7
  232.9 23.1 %collective-permute-start = (bf16[3,2,16,1024]{3,2,1,0:T(8,128)(2,1)S(1)}, bf16[3,2,16,1024]{3,2,1,0:T(8,128)(2,1)S(1)}, u32[]{:S(2)}, u32[]{:S(2)}) collective-permute-start(bf16[3,2,16,1024]{3,2,1,0:T(8,128)(2,1)S(1)} %get-tuple-element.365), channel_id=1, source_target_pairs={{2,0},{4,2},{6,4},{8,6},{10,8},{12,10},{14,12},{16,14},{18,16},{20... | collective-permute-start | bytes 589832 | tf_op jit(solution)/shard_map/while/body/eval_jaxpr/ppermute | solution.py:19
  239.6 16.4 %collective-permute-start.1 = (bf16[3,2,16,1024]{3,2,1,0:T(8,128)(2,1)S(1)}, bf16[3,2,16,1024]{3,2,1,0:T(8,128)(2,1)}, u32[]{:S(2)}, u32[]{:S(2)}) collective-permute-start(bf16[3,2,16,1024]{3,2,1,0:T(8,128)(2,1)S(1)} %get-tuple-element.365), channel_id=1, source_target_pairs={{0,2},{2,4},{4,6},{6,8},{8,10},{10,12},{12,14},{14,16},{16,18},{18... | collective-permute-start | bytes 589832 | tf_op jit(solution)/shard_map/while/body/eval_jaxpr/ppermute | solution.py:16
  257.0 2.4 copy-start.6
  257.1 2.4 copy-start.7
  269.2 23.1 %collective-permute-start = (bf16[3,2,16,1024]{3,2,1,0:T(8,128)(2,1)S(1)}, bf16[3,2,16,1024]{3,2,1,0:T(8,128)(2,1)S(1)}, u32[]{:S(2)}, u32[]{:S(2)}) collective-permute-start(bf16[3,2,16,1024]{3,2,1,0:T(8,128)(2,1)S(1)} %get-tuple-element.365), channel_id=1, source_target_pairs={{2,0},{4,2},{6,4},{8,6},{10,8},{12,10},{14,12},{16,14},{18,16},{20... | collective-permute-start | bytes 589832 | tf_op jit(solution)/shard_map/while/body/eval_jaxpr/ppermute | solution.py:19
  275.9 16.4 %collective-permute-start.1 = (bf16[3,2,16,1024]{3,2,1,0:T(8,128)(2,1)S(1)}, bf16[3,2,16,1024]{3,2,1,0:T(8,128)(2,1)}, u32[]{:S(2)}, u32[]{:S(2)}) collective-permute-start(bf16[3,2,16,1024]{3,2,1,0:T(8,128)(2,1)S(1)} %get-tuple-element.365), channel_id=1, source_target_pairs={{0,2},{2,4},{4,6},{6,8},{8,10},{10,12},{12,14},{14,16},{16,18},{18... | collective-permute-start | bytes 589832 | tf_op jit(solution)/shard_map/while/body/eval_jaxpr/ppermute | solution.py:16
  293.3 2.4 copy-start.6
  293.4 2.4 copy-start.7
  305.5 23.2 %collective-permute-start = (bf16[3,2,16,1024]{3,2,1,0:T(8,128)(2,1)S(1)}, bf16[3,2,16,1024]{3,2,1,0:T(8,128)(2,1)S(1)}, u32[]{:S(2)}, u32[]{:S(2)}) collective-permute-start(bf16[3,2,16,1024]{3,2,1,0:T(8,128)(2,1)S(1)} %get-tuple-element.365), channel_id=1, source_target_pairs={{2,0},{4,2},{6,4},{8,6},{10,8},{12,10},{14,12},{16,14},{18,16},{20... | collective-permute-start | bytes 589832 | tf_op jit(solution)/shard_map/while/body/eval_jaxpr/ppermute | solution.py:19
  312.3 16.4 %collective-permute-start.1 = (bf16[3,2,16,1024]{3,2,1,0:T(8,128)(2,1)S(1)}, bf16[3,2,16,1024]{3,2,1,0:T(8,128)(2,1)}, u32[]{:S(2)}, u32[]{:S(2)}) collective-permute-start(bf16[3,2,16,1024]{3,2,1,0:T(8,128)(2,1)S(1)} %get-tuple-element.365), channel_id=1, source_target_pairs={{0,2},{2,4},{4,6},{6,8},{8,10},{10,12},{12,14},{14,16},{16,18},{18... | collective-permute-start | bytes 589832 | tf_op jit(solution)/shard_map/while/body/eval_jaxpr/ppermute | solution.py:16
  329.8 2.4 copy-start.6
  329.8 2.4 copy-start.7
  342.0 23.1 %collective-permute-start = (bf16[3,2,16,1024]{3,2,1,0:T(8,128)(2,1)S(1)}, bf16[3,2,16,1024]{3,2,1,0:T(8,128)(2,1)S(1)}, u32[]{:S(2)}, u32[]{:S(2)}) collective-permute-start(bf16[3,2,16,1024]{3,2,1,0:T(8,128)(2,1)S(1)} %get-tuple-element.365), channel_id=1, source_target_pairs={{2,0},{4,2},{6,4},{8,6},{10,8},{12,10},{14,12},{16,14},{18,16},{20... | collective-permute-start | bytes 589832 | tf_op jit(solution)/shard_map/while/body/eval_jaxpr/ppermute | solution.py:19
  348.6 16.4 %collective-permute-start.1 = (bf16[3,2,16,1024]{3,2,1,0:T(8,128)(2,1)S(1)}, bf16[3,2,16,1024]{3,2,1,0:T(8,128)(2,1)}, u32[]{:S(2)}, u32[]{:S(2)}) collective-permute-start(bf16[3,2,16,1024]{3,2,1,0:T(8,128)(2,1)S(1)} %get-tuple-element.365), channel_id=1, source_target_pairs={{0,2},{2,4},{4,6},{6,8},{8,10},{10,12},{12,14},{14,16},{16,18},{18... | collective-permute-start | bytes 589832 | tf_op jit(solution)/shard_map/while/body/eval_jaxpr/ppermute | solution.py:16
  366.0 2.4 copy-start.6
  366.1 2.4 copy-start.7
  378.2 23.2 %collective-permute-start = (bf16[3,2,16,1024]{3,2,1,0:T(8,128)(2,1)S(1)}, bf16[3,2,16,1024]{3,2,1,0:T(8,128)(2,1)S(1)}, u32[]{:S(2)}, u32[]{:S(2)}) collective-permute-start(bf16[3,2,16,1024]{3,2,1,0:T(8,128)(2,1)S(1)} %get-tuple-element.365), channel_id=1, source_target_pairs={{2,0},{4,2},{6,4},{8,6},{10,8},{12,10},{14,12},{16,14},{18,16},{20... | collective-permute-start | bytes 589832 | tf_op jit(solution)/shard_map/while/body/eval_jaxpr/ppermute | solution.py:19
  385.0 16.5 %collective-permute-start.1 = (bf16[3,2,16,1024]{3,2,1,0:T(8,128)(2,1)S(1)}, bf16[3,2,16,1024]{3,2,1,0:T(8,128)(2,1)}, u32[]{:S(2)}, u32[]{:S(2)}) collective-permute-start(bf16[3,2,16,1024]{3,2,1,0:T(8,128)(2,1)S(1)} %get-tuple-element.365), channel_id=1, source_target_pairs={{0,2},{2,4},{4,6},{6,8},{8,10},{10,12},{12,14},{14,16},{16,18},{18... | collective-permute-start | bytes 589832 | tf_op jit(solution)/shard_map/while/body/eval_jaxpr/ppermute | solution.py:16
  402.4 2.4 copy-start.6
  402.5 2.4 copy-start.7
  414.6 23.0 %collective-permute-start = (bf16[3,2,16,1024]{3,2,1,0:T(8,128)(2,1)S(1)}, bf16[3,2,16,1024]{3,2,1,0:T(8,128)(2,1)S(1)}, u32[]{:S(2)}, u32[]{:S(2)}) collective-permute-start(bf16[3,2,16,1024]{3,2,1,0:T(8,128)(2,1)S(1)} %get-tuple-element.365), channel_id=1, source_target_pairs={{2,0},{4,2},{6,4},{8,6},{10,8},{12,10},{14,12},{16,14},{18,16},{20... | collective-permute-start | bytes 589832 | tf_op jit(solution)/shard_map/while/body/eval_jaxpr/ppermute | solution.py:19
  421.2 16.4 %collective-permute-start.1 = (bf16[3,2,16,1024]{3,2,1,0:T(8,128)(2,1)S(1)}, bf16[3,2,16,1024]{3,2,1,0:T(8,128)(2,1)}, u32[]{:S(2)}, u32[]{:S(2)}) collective-permute-start(bf16[3,2,16,1024]{3,2,1,0:T(8,128)(2,1)S(1)} %get-tuple-element.365), channel_id=1, source_target_pairs={{0,2},{2,4},{4,6},{6,8},{8,10},{10,12},{12,14},{14,16},{16,18},{18... | collective-permute-start | bytes 589832 | tf_op jit(solution)/shard_map/while/body/eval_jaxpr/ppermute | solution.py:16
  438.7 2.4 copy-start.6
  438.7 2.4 copy-start.7
  450.9 23.1 %collective-permute-start = (bf16[3,2,16,1024]{3,2,1,0:T(8,128)(2,1)S(1)}, bf16[3,2,16,1024]{3,2,1,0:T(8,128)(2,1)S(1)}, u32[]{:S(2)}, u32[]{:S(2)}) collective-permute-start(bf16[3,2,16,1024]{3,2,1,0:T(8,128)(2,1)S(1)} %get-tuple-element.365), channel_id=1, source_target_pairs={{2,0},{4,2},{6,4},{8,6},{10,8},{12,10},{14,12},{16,14},{18,16},{20... | collective-permute-start | bytes 589832 | tf_op jit(solution)/shard_map/while/body/eval_jaxpr/ppermute | solution.py:19
  457.6 16.4 %collective-permute-start.1 = (bf16[3,2,16,1024]{3,2,1,0:T(8,128)(2,1)S(1)}, bf16[3,2,16,1024]{3,2,1,0:T(8,128)(2,1)}, u32[]{:S(2)}, u32[]{:S(2)}) collective-permute-start(bf16[3,2,16,1024]{3,2,1,0:T(8,128)(2,1)S(1)} %get-tuple-element.365), channel_id=1, source_target_pairs={{0,2},{2,4},{4,6},{6,8},{8,10},{10,12},{12,14},{14,16},{16,18},{18... | collective-permute-start | bytes 589832 | tf_op jit(solution)/shard_map/while/body/eval_jaxpr/ppermute | solution.py:16
  475.0 2.4 copy-start.6
  475.0 2.4 copy-start.7
